TPU v7x, 128 devices: a whole 4x4x4 slice. The times are simulated.
128 devices in a mesh: row: 8 (over y_lo, z), col: 16 (over y_hi, x, core).
Axes of the slice: x: 4, y: 4 (y_hi: 2, y_lo: 2; y = y_hi * 2 + y_lo), z: 4, core: 2. Of those that a mesh axis runs over, the one named last changes fastest.
Arguments:
- ocean_state: float32 [1024, 24, 4096], P('row', None, 'col'), may hold values from -6 to 6
- saved_checksums: float32 [1024, 4, 24, 256], P(('row', 'col')), may hold values from -24 to 24
- checksum_weights: int32 [4, 16], replicated, may hold values from 1 to 3
- failed_devices: int32 [8, 2], replicated, may hold values from 0 to 15, as said below
- column_op: float32 [24, 24], replicated, may hold values from -1.25 to 1.25
- diffusivity: float32 [24], replicated, may hold values from 0.04 to 0.2
Outputs:
- stepped_state: float32 [1024, 24, 4096], P('row', None, 'col')
- fresh_parity: float32 [1024, 4, 24, 256], P(('row', 'col'))
Inputs may be any that keep to these rules, and one draw needn't show every extreme that they name: `failed_devices`: the two entries of a row differ.
All inputs are finite; a program needn't handle non-finite values.
Results may differ from a plain program's by a relative error of at most 0.00022.
Values sent between devices are 32-bit elements; how exact they have to be, the bound alone decides.
No kernel may reach another device: no remote copies, remote signals or barrier semaphores. Data moves between devices by JAX's collectives and lax.ppermute only.
A program may use at most 64 MiB of HBM per device.

v0:
```python
import functools

import jax
import jax.numpy as jnp
from jax import lax
from jax.experimental import pallas as pl
from jax.experimental.pallas import tpu as pltpu
from jax.sharding import PartitionSpec as P

CHUNK_PAIRS = 2
VMEM_BYTES = 20 * 1024 * 1024
SMEM = pl.BlockSpec(memory_space=pltpu.SMEM)
VMEM = pl.BlockSpec(memory_space=pltpu.VMEM)

GROUP = 8
MEMBERS = ("y_hi", "x", "core")


def column(weights, member):
    return [weights[k, member] for k in range(weights.shape[0])]


def dot(left, right):
    return sum(x * y for x, y in zip(left, right))


def rebuild_kernel(
    failed, weights, strips, saved, parity, rebuilt, back, shared, edges, factors, fresh, sem
):
    count, rows, fields, columns = strips.shape
    checks = saved.shape[1]
    half = columns // 2
    wide = 2 * fields
    lane = lax.broadcasted_iota(jnp.int32, (fields, half), 1)
    edges[...] = jnp.zeros_like(edges)
    line = lax.axis_index("row")
    lost = (failed[0, line], failed[1, line])

    any_shared = jnp.int32(0)
    for r in range(failed.shape[1]):
        any_shared |= (failed[0, r] // 2 == failed[1, r] // 2).astype(jnp.int32)
    shared[0] = any_shared

    u, v = column(weights, lost[0]), column(weights, lost[1])
    gram_aa, gram_bb, gram_ab = dot(u, u) + 1, dot(v, v) + 1, dot(u, v)
    determinant = (gram_aa * gram_bb - gram_ab * gram_ab).astype(jnp.float32)
    scale = 1.0 / jnp.full((fields, columns), determinant, jnp.float32)
    for c in range(count):
        kept = ((lost[0] != c) & (lost[1] != c)).astype(jnp.int32)
        for k in range(checks):
            factors[k, c] = (kept * weights[k, c]).astype(jnp.float32)
    for k in range(checks):
        factors[k, count] = u[k].astype(jnp.float32)
        factors[k, count + 1] = v[k].astype(jnp.float32)
        factors[k, count + 2] = (gram_bb * u[k] - gram_ab * v[k]).astype(jnp.float32)
        factors[k, count + 3] = (gram_aa * v[k] - gram_ab * u[k]).astype(jnp.float32)

    def keep_edges(n, i, first, final):
        ends = pltpu.roll(jnp.where(lane == 0, first, final), 2 * i + 1, 1)
        edges[n] = jnp.where((lane == 2 * i) | (lane == 2 * i + 1), ends, edges[n])

    @pl.loop(0, rows)
    def _(i):
        at = pl.multiple_of(i * wide, 8)
        living = [None] * checks
        for c in range(count):
            block = strips[c, i]
            keep_edges(c, i, block[:, :half], block[:, half:])
            for k in range(checks):
                term = factors[k, c] * block
                living[k] = term if c == 0 else living[k] + term
        whole = [None, None]
        for k in range(checks):
            residue = saved[i, k] - living[k]
            for b in range(2):
                term = factors[k, count + 2 + b] * residue
                whole[b] = term if k == 0 else whole[b] + term
        whole = [x * scale for x in whole]
        for k in range(checks):
            fresh[i, k] = (
                living[k] + factors[k, count] * whole[0] + factors[k, count + 1] * whole[1]
            )
        pltpu.make_async_copy(fresh.at[i], parity.at[i], sem.at[i]).start()
        for b in range(2):
            first, final = whole[b][:, :half], whole[b][:, half:]
            keep_edges(count + b, i, first, final)
            whole[b] = jnp.concatenate([first, final], axis=0)
            rebuilt[b, pl.ds(at, wide), :] = whole[b]
        for c in range(count // 2):
            chosen = jnp.where(lost[0] // 2 == c, whole[0], whole[1])
            back[c, pl.ds(at + GROUP, wide), :] = chosen

    def recovered_edges(c):
        if c < 0 or c >= count:
            return jnp.zeros((fields, half), jnp.float32)
        raw = jnp.where(lost[1] == c, edges[count + 1], edges[c])
        return jnp.where(lost[0] == c, edges[count], raw)

    for c in range(0, count, 2):
        near = [recovered_edges(c + d) for d in (-1, 0, 1, 2)]
        both = jnp.where(lane % 2 == 0, near[0], near[2])
        both = both + pltpu.roll(jnp.where(lane % 2 == 0, near[1], near[3]), 2 * rows, 1)
        packed = both[:GROUP]
        for g in range(1, fields // GROUP):
            packed = packed + pltpu.roll(both[g * GROUP : (g + 1) * GROUP], 4 * rows * g, 1)
        back[c // 2, 0:GROUP, :] = packed
    for i in range(rows):
        pltpu.make_async_copy(fresh.at[i], parity.at[i], sem.at[i]).wait()


def rebuild(failed, weights, strips, saved):
    count, rows, fields, columns = strips.shape
    half = columns // 2
    whole = 2 * rows * fields
    checks = weights.shape[0]
    return pl.pallas_call(
        rebuild_kernel,
        out_shape=(
            jax.ShapeDtypeStruct(saved.shape, jnp.float32),
            jax.ShapeDtypeStruct((2, whole, half), jnp.float32),
            jax.ShapeDtypeStruct((count // 2, GROUP + whole, half), jnp.float32),
            jax.ShapeDtypeStruct((1,), jnp.int32),
        ),
        in_specs=[SMEM, SMEM, VMEM, VMEM],
        out_specs=(pl.BlockSpec(memory_space=pl.ANY), VMEM, VMEM, SMEM),
        scratch_shapes=[
            pltpu.VMEM((count + 2, fields, half), jnp.float32),
            pltpu.SMEM((checks, count + 4), jnp.float32),
            pltpu.VMEM(saved.shape, jnp.float32),
            pltpu.SemaphoreType.DMA((rows,)),
        ],
        compiler_params=pltpu.CompilerParams(vmem_limit_bytes=VMEM_BYTES),
        cost_estimate=pl.CostEstimate(
            flops=8 * strips.size, bytes_accessed=6 * strips.size, transcendentals=0
        ),
    )(failed, weights, strips, saved)


def spread_kernel(failed, rebuilt, short, back):
    lost_a = failed[0, lax.axis_index("row")]
    for c in range(back.shape[0]):
        back[c, 0:GROUP, :] = short[c // 2, 0:GROUP, :]
        back[c, GROUP:, :] = jnp.where(lost_a == c, rebuilt[0], rebuilt[1])


def spread_whole(failed, rebuilt, short):
    chips, lines, half = short.shape
    return pl.pallas_call(
        spread_kernel,
        out_shape=jax.ShapeDtypeStruct((2 * chips, lines, half), jnp.float32),
        in_specs=[SMEM, VMEM, VMEM],
        out_specs=VMEM,
        compiler_params=pltpu.CompilerParams(vmem_limit_bytes=VMEM_BYTES),
    )(failed, rebuilt, short)


def beside(cells):
    half = cells.shape[0] // 2
    return jnp.concatenate([cells[:half], cells[half:]], axis=1)


def below(cells):
    half = cells.shape[1] // 2
    return jnp.concatenate([cells[:, :half], cells[:, half:]], axis=0)


def mix_pair(operator, flat):
    high = flat.astype(jnp.bfloat16)
    low = (flat - high.astype(jnp.float32)).astype(jnp.bfloat16)
    terms = jnp.concatenate([high, low, high], axis=0)
    return flat + jnp.tanh(jnp.dot(operator[...], terms, preferred_element_type=jnp.float32))


def mix_strip(operator, lost, sent, base, ocean, strip, store):
    fields, columns = ocean.shape[1:]
    wide = 2 * fields
    head = None
    for t in range(0, strip, 2):
        units = []
        for q in (t, t + 1):
            own = slice(GROUP + q * wide, GROUP + (q + 1) * wide)
            units.append(jnp.where(lost, beside(sent(own)), ocean[base + q]))
        done = mix_pair(operator, jnp.concatenate(units, axis=0)).reshape(2, fields, columns)
        store(t, done)
        if t == 0:
            head = done[0]
    return head


def my_place(failed):
    line = lax.axis_index("row")
    member = lax.axis_index(MEMBERS)
    lost = (failed[0, line] == member) | (failed[1, line] == member)
    return line, member, member % 2, lost


def double_operator(op):
    fields = op.shape[0]
    wide = 2 * fields
    tall = lax.broadcasted_iota(jnp.int32, (wide, fields), 0) % fields
    tall = (tall == lax.broadcasted_iota(jnp.int32, (wide, fields), 1)).astype(jnp.float32)
    flat = lax.broadcasted_iota(jnp.int32, (fields, wide), 1) % fields
    flat = (flat == lax.broadcasted_iota(jnp.int32, (fields, wide), 0)).astype(jnp.float32)
    exact = dict(preferred_element_type=jnp.float32, precision=lax.Precision.HIGHEST)
    tiled = jnp.dot(jnp.dot(tall, op[...], **exact), flat, **exact)
    down = lax.broadcasted_iota(jnp.int32, (wide, wide), 0) // fields
    across = lax.broadcasted_iota(jnp.int32, (wide, wide), 1) // fields
    both = jnp.where(down == across, tiled, 0.0)
    high = both.astype(jnp.bfloat16)
    low = (both - high.astype(jnp.float32)).astype(jnp.bfloat16)
    return jnp.concatenate([high, high, low], axis=1)


def rows_kernel(whole, failed, ocean, *refs):
    *sent, row_top, row_bottom = refs
    rows, fields, columns = ocean.shape
    wide = 2 * fields
    last = sent[0].shape[0] - 1
    first = slice(GROUP, GROUP + wide)
    final = slice(sent[0].shape[1] - wide, sent[0].shape[1])
    _, _, core, lost = my_place(failed)
    if whole:
        top, bottom = sent[0][0, first, :], sent[0][last, final, :]
    else:
        mine, other = sent
        top = jnp.where(core == 0, mine[0, first, :], other[0, first, :])
        bottom = jnp.where(core == 0, other[last, final, :], mine[last, final, :])
    row_top[...] = jnp.where(lost, top, below(ocean[0]))
    row_bottom[...] = jnp.where(lost, bottom, below(ocean[rows - 1]))


def outer_lines(failed, ocean, sent):
    rows, fields, columns = ocean.shape
    line = jax.ShapeDtypeStruct((2 * fields, columns // 2), jnp.float32)
    return pl.pallas_call(
        functools.partial(rows_kernel, len(sent) == 1),
        out_shape=(line, line),
        in_specs=[SMEM] + [VMEM] * (1 + len(sent)),
        out_specs=(VMEM, VMEM),
        compiler_params=pltpu.CompilerParams(vmem_limit_bytes=VMEM_BYTES),
    )(failed, ocean, *sent)


def first_kernel(whole, failed, ocean, sent, op, diffusivity, strips, operator, number_of):
    rows, fields, columns = ocean.shape
    half = columns // 2
    count = 2 * strips.shape[0]
    strip = rows // count
    _, _, core, lost = my_place(failed)
    operator[...] = double_operator(op)
    field = lax.broadcasted_iota(jnp.int32, (fields, half), 0)
    number = jnp.zeros((fields, half), jnp.float32)
    for f in range(fields):
        number = jnp.where(field == f, diffusivity[f], number)
    number_of[...] = number

    @pl.loop(0, count // 2)
    def _(p):
        s = 2 * p + core
        at = s if whole else p

        def store(t, done):
            strips[p, pl.ds(t, 2)] = done

        base = pl.multiple_of(s * strip, strip)
        mix_strip(operator, lost, lambda own: sent[at, own, :], base, ocean, strip, store)


def first_half(failed, ocean, sent, op, diffusivity, whole, count):
    rows, fields, columns = ocean.shape
    half = columns // 2
    wide = 2 * fields
    shapes = [jax.ShapeDtypeStruct((count // 2, rows // count, fields, columns), jnp.float32)]
    shapes.append(jax.ShapeDtypeStruct((wide, 3 * wide), jnp.bfloat16))
    shapes.append(jax.ShapeDtypeStruct((fields, half), jnp.float32))
    return pl.pallas_call(
        functools.partial(first_kernel, whole),
        out_shape=tuple(shapes),
        in_specs=[SMEM, VMEM, VMEM, VMEM, SMEM],
        out_specs=(VMEM,) * len(shapes),
        compiler_params=pltpu.CompilerParams(vmem_limit_bytes=VMEM_BYTES),
        cost_estimate=pl.CostEstimate(
            flops=75 * ocean.size, bytes_accessed=4 * ocean.size, transcendentals=ocean.size // 2
        ),
    )(failed, ocean, sent, op, diffusivity)


def step_kernel(whole, failed, ocean, *refs):
    if whole:
        sent, strips, operator, number_of, *refs = refs
    else:
        mine, other, strips, operator, number_of, *refs = refs
    out, mixed, sides = refs
    rows, fields, columns = ocean.shape
    half = columns // 2
    wide = 2 * fields
    pairs = strips.shape[0]
    count = 2 * pairs
    strip = rows // count
    step = pl.program_id(0)
    _, _, core, lost = my_place(failed)
    lane = lax.broadcasted_iota(jnp.int32, (fields, half), 1)
    number = number_of[...]

    def prepare(p):
        kept = pl.multiple_of((2 * p + core) * strip, strip)
        base = pl.multiple_of((2 * p + 1 - core) * strip, strip)
        at = 2 * p + 1 - core if whole else p
        source = sent if whole else other
        for t in range(0, strip, 2):
            mixed[pl.ds(kept + t + 1, 2)] = strips[p, pl.ds(t, 2)]

        def store(t, done):
            mixed[pl.ds(base + t + 1, 2)] = done

        head = mix_strip(operator, lost, lambda own: source[at, own, :], base, ocean, strip, store)
        return jnp.where(core == 0, strips[p, 0], head)

    def tile_of(s):
        if whole:
            return sent[s, 0:GROUP, :]
        return jnp.where(core == s % 2, mine[s // 2, 0:GROUP, :], other[s // 2, 0:GROUP, :])

    @pl.when(step == 0)
    def _():
        mixed[0] = jnp.zeros((fields, columns), jnp.float32)
        mixed[rows + 1] = jnp.zeros((fields, columns), jnp.float32)
        narrow = lane[:GROUP]
        ends = []
        for g in range(fields // GROUP):
            parts = []
            for h in range(2):
                part = jnp.zeros((GROUP, half), jnp.float32)
                for n in range(count // 2):
                    tile = tile_of(h * count // 2 + n)
                    shift = (2 * strip * (n - 2 * g)) % half
                    near = pltpu.roll(tile, shift, 1) if shift else tile
                    shift = (2 * strip * (n - 2 * g - 1)) % half
                    far = pltpu.roll(tile, shift, 1) if shift else tile
                    part = jnp.where(
                        narrow // (2 * strip) == n, jnp.where(core == 0, near, far), part
                    )
                parts.append(part)
            ends.append(jnp.concatenate(parts, axis=1))
        ends = jnp.concatenate(ends, axis=0)
        ends = mix_pair(operator, jnp.concatenate([ends, ends], axis=0))[:fields]
        for h in range(2):
            part = ends[:, h * half : (h + 1) * half]
            part = jnp.where(lane % 2 == 0, pltpu.roll(part, half - 1, 1), pltpu.roll(part, 1, 1))
            for n in range(count // 2):
                sides[h * count // 2 + n] = pltpu.roll(part, half - 2 * strip * n, 1) if n else part
        prepare(0)

    def diffuse(s, t, at, under_row):
        i = s * strip + t + 1
        side = pltpu.roll(sides[s], half - 2 * t - 1, 1)
        for part in range(2):
            own = slice(part * half, (part + 1) * half)
            here = mixed[i, :, own]
            across = mixed[i, :, (1 - part) * half : (2 - part) * half]
            if part == 0:
                west = jnp.where(lane == 0, side, pltpu.roll(here, 1, 1))
                east = pltpu.roll(jnp.where(lane == 0, across, here), half - 1, 1)
            else:
                west = pltpu.roll(jnp.where(lane == half - 1, across, here), 1, 1)
                east = jnp.where(lane == half - 1, side, pltpu.roll(here, half - 1, 1))
            under = mixed[i + 1, :, own] if under_row is None else under_row[:, own]
            around = under + mixed[i - 1, :, own] + east + west
            out[at, :, own] = here + number * (around - 4.0 * here)

    @pl.loop(0, CHUNK_PAIRS)
    def _(j):
        p = step * CHUNK_PAIRS + j
        for t in range(2 * strip - 1):
            diffuse(2 * p + t // strip, t % strip, 2 * strip * j + t, None)
        head = prepare(jnp.minimum(p + 1, pairs - 1))
        head = jnp.where(p == pairs - 1, mixed[rows + 1], head)
        diffuse(2 * p + 1, strip - 1, 2 * strip * (j + 1) - 1, head)


def step(failed, ocean, sent, strips, operator, number_of):
    rows, fields, columns = ocean.shape
    whole = len(sent) == 1
    pairs = strips.shape[0]
    chunk = CHUNK_PAIRS * rows // pairs
    return pl.pallas_call(
        functools.partial(step_kernel, whole),
        grid=(rows // chunk,),
        out_shape=jax.ShapeDtypeStruct(ocean.shape, jnp.float32),
        in_specs=[SMEM] + [VMEM] * (4 + len(sent)),
        out_specs=pl.BlockSpec((chunk, fields, columns), lambda g: (g, 0, 0)),
        scratch_shapes=[
            pltpu.VMEM((rows + 2, fields, columns), jnp.float32),
            pltpu.VMEM((2 * pairs, fields, columns // 2), jnp.float32),
        ],
        compiler_params=pltpu.CompilerParams(
            vmem_limit_bytes=VMEM_BYTES, dimension_semantics=("arbitrary",)
        ),
        cost_estimate=pl.CostEstimate(
            flops=100 * ocean.size, bytes_accessed=12 * ocean.size, transcendentals=ocean.size // 2
        ),
    )(failed, ocean, *sent, strips, operator, number_of)


def ends_kernel(stepped, above, under, operator, number_of, out, row, sem):
    rows, fields, columns = stepped.shape
    places = (0, rows - 1)
    reads = [
        pltpu.make_async_copy(out.at[at], row.at[n], sem.at[n]) for n, at in enumerate(places)
    ]
    for copy in reads:
        copy.start()
    both = jnp.concatenate([beside(above[...]), beside(under[...])], axis=0)
    both = mix_pair(operator, both)
    number = jnp.concatenate([number_of[...], number_of[...]], axis=1)
    writes = []
    for n, at in enumerate(places):
        reads[n].wait()
        row[n] = row[n] + number * both[n * fields : (n + 1) * fields]
        writes.append(pltpu.make_async_copy(row.at[n], out.at[at], sem.at[n]))
        writes[n].start()
    for copy in writes:
        copy.wait()


def add_ends(stepped, above, under, operator, number_of):
    rows, fields, columns = stepped.shape
    anywhere = pl.BlockSpec(memory_space=pl.ANY)
    return pl.pallas_call(
        ends_kernel,
        out_shape=jax.ShapeDtypeStruct(stepped.shape, jnp.float32),
        in_specs=[anywhere] + [VMEM] * 4,
        out_specs=anywhere,
        input_output_aliases={0: 0},
        scratch_shapes=[
            pltpu.VMEM((2, fields, columns), jnp.float32),
            pltpu.SemaphoreType.DMA((2,)),
        ],
        compiler_params=pltpu.CompilerParams(vmem_limit_bytes=VMEM_BYTES),
    )(stepped, above, under, operator, number_of)


def per_device(
    ocean_state, saved_checksums, checksum_weights, failed_devices, column_op, diffusivity
):
    lines = lax.axis_size("row")
    rows, fields, columns = ocean_state.shape
    count = checksum_weights.shape[1]
    half = columns // 2
    strip = rows // count

    strips = lax.all_to_all(ocean_state, MEMBERS, 0, 0, tiled=True)
    strips, ocean, saved, weights, failed, op, number = lax.optimization_barrier(
        (
            strips,
            ocean_state,
            saved_checksums,
            checksum_weights,
            failed_devices.T,
            column_op,
            diffusivity,
        )
    )
    strips = strips.reshape(count, strip, fields, columns)
    fresh_parity, rebuilt, back, shared = rebuild(failed, weights, strips, saved)

    def finish(ocean, sent, kept):
        top, bottom = outer_lines(failed, ocean, sent)
        above = lax.ppermute(bottom, "row", [(r, r + 1) for r in range(lines - 1)])
        under = lax.ppermute(top, "row", [(r + 1, r) for r in range(lines - 1)])
        stepped = step(failed, ocean, sent, *kept)
        return add_ends(stepped, above, under, *kept[1:])

    def exchange_chips(rebuilt, back, ocean):
        mine = lax.all_to_all(back, ("y_hi", "x"), 0, 0, tiled=True)
        mine, ocean = lax.optimization_barrier((mine, ocean))
        other = lax.ppermute(mine, "core", [(0, 1), (1, 0)])
        kept = first_half(failed, ocean, mine, op, number, False, count)
        other, kept = lax.optimization_barrier((other, kept))
        return finish(ocean, (mine, other), kept)

    def exchange_whole(rebuilt, back, ocean):
        back = spread_whole(failed, rebuilt, back)
        sent = lax.all_to_all(back, MEMBERS, 0, 0, tiled=True)
        sent, ocean = lax.optimization_barrier((sent, ocean))
        kept = first_half(failed, ocean, sent, op, number, True, count)
        return finish(ocean, (sent,), kept)

    stepped_state = lax.cond(
        shared[0] != 0, exchange_whole, exchange_chips, rebuilt, back, ocean
    )
    return stepped_state, fresh_parity


def solution(mesh):
    row, col = mesh.axis_names
    shape = (mesh.shape[row], 2, 4, 2)
    chips = jax.sharding.Mesh(mesh.devices.reshape(shape), ("row", "y_hi", "x", "core"))
    col = MEMBERS
    return jax.shard_map(
        per_device,
        mesh=chips,
        in_specs=(P("row", None, col), P(("row", *col), None, None, None), P(), P(), P(), P()),
        out_specs=(P("row", None, col), P(("row", *col), None, None, None)),
        check_vma=False,
    )
```

profile of v0, /device:TPU:15, one launch (start us, length us, event | category | flops | bytes accessed | tf_op | source)
XLA Modules:
  0.0 113.3 jit_solution(444308413051341692)
XLA Ops:
  0.6 0.0 copy-start.3
  0.6 0.0 copy-start.1
  0.7 0.0 copy-start
  0.7 45.1 %all_to_all.15 = f32[128,24,256]{2,1,0:T(8,128)S(1)} all-to-all(f32[128,24,256]{2,1,0:T(8,128)} %param.8), channel_id=1, replica_groups=mesh['row'=8,'y_hi'=2,'x'=4,'core'=2] {'y_hi','x','core'}, dimensions={0} | all-to-all | bytes 6291456 | tf_op jit(solution)/shard_map/all_to_all | solution.py:452
  45.7 0.0 copy-start.2
  45.7 0.0 copy-start.4
  45.7 0.0 copy-start.5
  45.7 0.0 copy-done.3
  45.7 0.0 copy-done.1
  45.8 0.0 copy-done
  45.8 3.8 %shard_map.77 = (f32[8,4,24,256]{3,2,1,0:T(8,128)}, f32[2,384,128]{2,1,0:T(8,128)S(1)}, f32[8,392,128]{2,1,0:T(8,128)S(1)}, s32[1]{0:T(128)}) custom-call(s32[2,8]{1,0:T(2,128)S(1)} %bitcast.4, s32[4,16]{1,0:T(4,128)S(1)} %copy-done.1, f32[16,8,24,256]{3,2,1,0:T(8,128)S(1)} %bitcast.3, f32[8,4,24,256]{3,2,1,0:T(8,128)S(1)} %copy-done), custom_call_target="tpu_custom_call" | custom-call | flops 6291456 | bytes 4718592 | tf_op jit(solution)/shard_map/pallas_call | solution.py:116
  50.2 0.0 copy-done.2
  50.2 0.0 copy-done.4
  50.2 0.0 copy-done.5
  50.3 63.0 %conditional.1 = (f32[128,24,256]{2,1,0:T(8,128)}) conditional(s32[]{:T(128)} %bitcast.2, (f32[8,392,128]{2,1,0:T(8,128)S(1)}, f32[128,24,256]{2,1,0:T(8,128)S(1)}, s32[2,8]{1,0:T(2,128)S(1)}, f32[24,24]{1,0:T(8,128)S(1)}, f32[24]{0:T(128)S(1)}) %tuple.30, (s32[2,8]{1,0:T(2,128)S(1)}, f32[2,384,128]{2,1,0:T(8,128)S(1)}, f32[8,392,128]{2,1,0:T(8,128)S(1)}, ...), branch_computations={%region_0.0_spmd, %region_1.0_spmd} | conditional | flops 137625600 | bytes 22413440 | solution.py:489
  50.3 0.8 branch_1_fun.5
  51.1 44.2 %all_to_all.14.sent.refs_0_ = f32[16,392,128]{2,1,0:T(8,128)S(1)} all-to-all(f32[16,392,128]{2,1,0:T(8,128)S(1)} %branch_1_fun.5), channel_id=1, replica_groups=mesh['row'=8,'y_hi'=2,'x'=4,'core'=2] {'y_hi','x','core'}, dimensions={0} | all-to-all | bytes 6422528 | tf_op jit(solution)/shard_map/cond/branch_1_fun/all_to_all | solution.py:484
  95.3 0.6 branch_1_fun.8
  95.9 3.5 %collective-permute-start.3 = (f32[48,128]{1,0:T(8,128)S(1)}, f32[48,128]{1,0:T(8,128)S(1)}, u32[]{:S(2)}, u32[]{:S(2)}) collective-permute-start(f32[48,128]{1,0:T(8,128)S(1)} %get-tuple-element.52), channel_id=1, source_target_pairs={{0,16},{16,32},{32,48},{48,64},{64,80},{80,96},{96,112},{1,17},{17... | collective-permute-start | bytes 73736 | tf_op jit(solution)/shard_map/cond/branch_1_fun/ppermute | solution.py:469
  99.4 4.8 %collective-permute-start.4 = (f32[48,128]{1,0:T(8,128)S(1)}, f32[48,128]{1,0:T(8,128)S(1)}, u32[]{:S(2)}, u32[]{:S(2)}) collective-permute-start(f32[48,128]{1,0:T(8,128)S(1)} %get-tuple-element.53), channel_id=1, source_target_pairs={{16,0},{32,16},{48,32},{64,48},{80,64},{96,80},{112,96},{17,1},{33... | collective-permute-start | bytes 73736 | tf_op jit(solution)/shard_map/cond/branch_1_fun/ppermute | solution.py:470
  104.3 2.5 %branch_1_fun.6 = (f32[8,8,24,256]{3,2,1,0:T(8,128)S(1)}, bf16[48,144]{1,0:T(8,128)(2,1)S(1)}, f32[24,128]{1,0:T(8,128)S(1)}) custom-call(s32[2,8]{1,0:T(2,128)S(1)} %get-tuple-element.41.failed, f32[128,24,256]{2,1,0:T(8,128)S(1)} %get-tuple-element.45.ocean, f32[16,392,128]{2,1,0:T(8,128)S(1)} %all_to_all.14.sent.refs_0_, ...), custom_call_target="tpu_custom_call" | custom-call | flops 58982400 | bytes 3145728 | tf_op jit(solution)/shard_map/cond/branch_1_fun/pallas_call | solution.py:276
  106.8 5.1 %branch_1_fun.7.stepped = f32[128,24,256]{2,1,0:T(8,128)} custom-call(s32[2,8]{1,0:T(2,128)S(1)} %get-tuple-element.41.failed, f32[128,24,256]{2,1,0:T(8,128)S(1)} %get-tuple-element.45.ocean, f32[16,392,128]{2,1,0:T(8,128)S(1)} %all_to_all.14.sent.refs_0_, f32[8,8,24,256]{3,2,1,0:T(8,128)S(1)} %get-tuple-element.49.refs_1_, ...), custom_call_target="tpu_custom_call" | custom-call | flops 78643200 | bytes 9437184 | tf_op jit(solution)/shard_map/cond/branch_1_fun/pallas_call | solution.py:386
  111.9 0.0 collective-permute-done.3.above
  111.9 0.0 collective-permute-done.4.under
  111.9 1.4 %branch_1_fun.9 = f32[128,24,256]{2,1,0:T(8,128)} custom-call(f32[128,24,256]{2,1,0:T(8,128)} %branch_1_fun.7.stepped, f32[48,128]{1,0:T(8,128)S(1)} %collective-permute-done.3.above, f32[48,128]{1,0:T(8,128)S(1)} %collective-permute-done.4.under, bf16[48,144]{1,0:T(8,128)(2,1)S(1)} %get-tuple-element.50.refs_2_.operator, ...), custom_call_target="tpu_custom_call", output_to_operand_aliasing={{}: (0, {})} | custom-call | tf_op jit(solution)/shard_map/cond/branch_1_fun/pallas_call | solution.py:429
Async XLA Ops:
  0.6 45.1 %copy-start.3 = (s32[8,2]{0,1:T(2,128)S(1)}, s32[8,2]{0,1:T(2,128)}, u32[]{:S(2)}) copy-start(s32[8,2]{0,1:T(2,128)} %param.11) | copy-start | bytes 196
  0.6 45.1 %copy-start.1 = (s32[4,16]{1,0:T(4,128)S(1)}, s32[4,16]{1,0:T(4,128)}, u32[]{:S(2)}) copy-start(s32[4,16]{1,0:T(4,128)} %weights) | copy-start | bytes 772
  0.7 45.1 %copy-start = (f32[8,4,24,256]{3,2,1,0:T(8,128)S(1)}, f32[8,4,24,256]{3,2,1,0:T(8,128)}, u32[]{:S(2)}) copy-start(f32[8,4,24,256]{3,2,1,0:T(8,128)} %saved) | copy-start | bytes 2359300
  45.7 4.5 %copy-start.2 = (f32[128,24,256]{2,1,0:T(8,128)S(1)}, f32[128,24,256]{2,1,0:T(8,128)}, u32[]{:S(2)}) copy-start(f32[128,24,256]{2,1,0:T(8,128)} %param.8) | copy-start | bytes 9437188
  45.7 4.5 %copy-start.4 = (f32[24,24]{1,0:T(8,128)S(1)}, f32[24,24]{1,0:T(8,128)}, u32[]{:S(2)}) copy-start(f32[24,24]{1,0:T(8,128)} %param.12) | copy-start | bytes 6916
  45.7 4.5 %copy-start.5 = (f32[24]{0:T(128)S(1)}, f32[24]{0:T(128)}, u32[]{:S(2)}) copy-start(f32[24]{0:T(128)} %param.13) | copy-start | bytes 292
  95.9 16.0 %collective-permute-start.3 = (f32[48,128]{1,0:T(8,128)S(1)}, f32[48,128]{1,0:T(8,128)S(1)}, u32[]{:S(2)}, u32[]{:S(2)}) collective-permute-start(f32[48,128]{1,0:T(8,128)S(1)} %get-tuple-element.52), channel_id=1, source_target_pairs={{0,16},{16,32},{32,48},{48,64},{64,80},{80,96},{96,112},{1,17},{17... | collective-permute-start | bytes 73736 | tf_op jit(solution)/shard_map/cond/branch_1_fun/ppermute | solution.py:469
  99.4 12.5 %collective-permute-start.4 = (f32[48,128]{1,0:T(8,128)S(1)}, f32[48,128]{1,0:T(8,128)S(1)}, u32[]{:S(2)}, u32[]{:S(2)}) collective-permute-start(f32[48,128]{1,0:T(8,128)S(1)} %get-tuple-element.53), channel_id=1, source_target_pairs={{16,0},{32,16},{48,32},{64,48},{80,64},{96,80},{112,96},{17,1},{33... | collective-permute-start | bytes 73736 | tf_op jit(solution)/shard_map/cond/branch_1_fun/ppermute | solution.py:470
where the time goes:
time: 115 us; the launch traced here: 113 us
  blocking collectives  89.2 us (78%)
  Pallas kernels  14.2 us (12%)
  starting transfers between devices  8.37 us (7%)
  between operations  1.36 us (1%)
    all_to_all x1, blocking collectives, per_device(): strips = lax.all_to_all(ocean_state, MEMBERS, 0, 0, tiled=True)  45.1 us
    all_to_all x1, blocking collectives, exchange_whole(): sent = lax.all_to_all(back, MEMBERS, 0, 0, tiled=True)  44.2 us
    pallas_call x1, Pallas kernels, step(): pl.pallas_call(functools.partial(step_kernel, whole), grid=(rows // chunk...  5.1 us
    ppermute x1, starting transfers between devices, finish(): under = lax.ppermute(top, 'row', [(r + 1, r) for r in range(lines - 1)])  4.83 us
    pallas_call x1, Pallas kernels, rebuild(): pl.pallas_call(rebuild_kernel, out_shape=(jax.ShapeDtypeStruct(saved.shap...  3.81 us
    ppermute x1, starting transfers between devices, finish(): above = lax.ppermute(bottom, 'row', [(r, r + 1) for r in range(lines - 1)])  3.55 us
    pallas_call x1, Pallas kernels, first_half(): pl.pallas_call(functools.partial(first_kernel, whole), out_shape=tuple(sh...  2.52 us
  transfers between devices with their start and end apart: 2, of which 0 were waited for; matrix products, arithmetic and copies ran while one was open for 0% of the time, Pallas kernels for 7%

commit v1 on v0

--- a/solution.py
+++ b/solution.py
@@ -7,7 +7,6 @@
 from jax.experimental.pallas import tpu as pltpu
 from jax.sharding import PartitionSpec as P
 
-CHUNK_PAIRS = 2
 VMEM_BYTES = 20 * 1024 * 1024
 SMEM = pl.BlockSpec(memory_space=pltpu.SMEM)
 VMEM = pl.BlockSpec(memory_space=pltpu.VMEM)
@@ -25,7 +24,7 @@
 
 
 def rebuild_kernel(
-    failed, weights, strips, saved, parity, rebuilt, back, shared, edges, factors, fresh, sem
+    failed, weights, strips, saved, fresh, rebuilt, back, shared, edges, factors
 ):
     count, rows, fields, columns = strips.shape
     checks = saved.shape[1]
@@ -80,7 +79,6 @@
             fresh[i, k] = (
                 living[k] + factors[k, count] * whole[0] + factors[k, count + 1] * whole[1]
             )
-        pltpu.make_async_copy(fresh.at[i], parity.at[i], sem.at[i]).start()
         for b in range(2):
             first, final = whole[b][:, :half], whole[b][:, half:]
             keep_edges(count + b, i, first, final)
@@ -104,8 +102,6 @@
         for g in range(1, fields // GROUP):
             packed = packed + pltpu.roll(both[g * GROUP : (g + 1) * GROUP], 4 * rows * g, 1)
         back[c // 2, 0:GROUP, :] = packed
-    for i in range(rows):
-        pltpu.make_async_copy(fresh.at[i], parity.at[i], sem.at[i]).wait()
 
 
 def rebuild(failed, weights, strips, saved):
@@ -122,12 +118,10 @@
             jax.ShapeDtypeStruct((1,), jnp.int32),
         ),
         in_specs=[SMEM, SMEM, VMEM, VMEM],
-        out_specs=(pl.BlockSpec(memory_space=pl.ANY), VMEM, VMEM, SMEM),
+        out_specs=(VMEM, VMEM, VMEM, SMEM),
         scratch_shapes=[
             pltpu.VMEM((count + 2, fields, half), jnp.float32),
             pltpu.SMEM((checks, count + 4), jnp.float32),
-            pltpu.VMEM(saved.shape, jnp.float32),
-            pltpu.SemaphoreType.DMA((rows,)),
         ],
         compiler_params=pltpu.CompilerParams(vmem_limit_bytes=VMEM_BYTES),
         cost_estimate=pl.CostEstimate(
@@ -241,7 +235,11 @@
     )(failed, ocean, *sent)
 
 
-def first_kernel(whole, failed, ocean, sent, op, diffusivity, strips, operator, number_of):
+def first_kernel(
+    whole, failed, ocean, sent, op, diffusivity, fresh, strips, operator, number_of, parity, sem
+):
+    leave = pltpu.make_async_copy(fresh, parity, sem)
+    leave.start()
     rows, fields, columns = ocean.shape
     half = columns // 2
     count = 2 * strips.shape[0]
@@ -265,29 +263,33 @@
         base = pl.multiple_of(s * strip, strip)
         mix_strip(operator, lost, lambda own: sent[at, own, :], base, ocean, strip, store)
 
-
-def first_half(failed, ocean, sent, op, diffusivity, whole, count):
+    leave.wait()
+
+
+def first_half(failed, ocean, sent, op, diffusivity, fresh, whole, count):
     rows, fields, columns = ocean.shape
     half = columns // 2
     wide = 2 * fields
     shapes = [jax.ShapeDtypeStruct((count // 2, rows // count, fields, columns), jnp.float32)]
     shapes.append(jax.ShapeDtypeStruct((wide, 3 * wide), jnp.bfloat16))
     shapes.append(jax.ShapeDtypeStruct((fields, half), jnp.float32))
+    shapes.append(jax.ShapeDtypeStruct(fresh.shape, jnp.float32))
     return pl.pallas_call(
         functools.partial(first_kernel, whole),
         out_shape=tuple(shapes),
-        in_specs=[SMEM, VMEM, VMEM, VMEM, SMEM],
-        out_specs=(VMEM,) * len(shapes),
+        in_specs=[SMEM, VMEM, VMEM, VMEM, SMEM, VMEM],
+        out_specs=(VMEM, VMEM, VMEM, pl.BlockSpec(memory_space=pl.ANY)),
+        scratch_shapes=[pltpu.SemaphoreType.DMA],
         compiler_params=pltpu.CompilerParams(vmem_limit_bytes=VMEM_BYTES),
         cost_estimate=pl.CostEstimate(
             flops=75 * ocean.size, bytes_accessed=4 * ocean.size, transcendentals=ocean.size // 2
         ),
-    )(failed, ocean, sent, op, diffusivity)
+    )(failed, ocean, sent, op, diffusivity, fresh)
 
 
 def step_kernel(whole, failed, ocean, *refs):
     if whole:
-        sent, strips, operator, number_of, *refs = refs
+        sent, strips, operator, number_of, above, under, *refs = refs
     else:
         mine, other, strips, operator, number_of, *refs = refs
     out, mixed, sides = refs
@@ -297,7 +299,6 @@
     pairs = strips.shape[0]
     count = 2 * pairs
     strip = rows // count
-    step = pl.program_id(0)
     _, _, core, lost = my_place(failed)
     lane = lax.broadcasted_iota(jnp.int32, (fields, half), 1)
     number = number_of[...]
@@ -321,37 +322,41 @@
             return sent[s, 0:GROUP, :]
         return jnp.where(core == s % 2, mine[s // 2, 0:GROUP, :], other[s // 2, 0:GROUP, :])
 
-    @pl.when(step == 0)
-    def _():
+    if whole:
+        outer = jnp.concatenate([beside(above[...]), beside(under[...])], axis=0)
+        outer = mix_pair(operator, outer)
+        mixed[0] = outer[:fields]
+        mixed[rows + 1] = outer[fields:]
+    else:
         mixed[0] = jnp.zeros((fields, columns), jnp.float32)
         mixed[rows + 1] = jnp.zeros((fields, columns), jnp.float32)
-        narrow = lane[:GROUP]
-        ends = []
-        for g in range(fields // GROUP):
-            parts = []
-            for h in range(2):
-                part = jnp.zeros((GROUP, half), jnp.float32)
-                for n in range(count // 2):
-                    tile = tile_of(h * count // 2 + n)
-                    shift = (2 * strip * (n - 2 * g)) % half
-                    near = pltpu.roll(tile, shift, 1) if shift else tile
-                    shift = (2 * strip * (n - 2 * g - 1)) % half
-                    far = pltpu.roll(tile, shift, 1) if shift else tile
-                    part = jnp.where(
-                        narrow // (2 * strip) == n, jnp.where(core == 0, near, far), part
-                    )
-                parts.append(part)
-            ends.append(jnp.concatenate(parts, axis=1))
-        ends = jnp.concatenate(ends, axis=0)
-        ends = mix_pair(operator, jnp.concatenate([ends, ends], axis=0))[:fields]
+    narrow = lane[:GROUP]
+    ends = []
+    for g in range(fields // GROUP):
+        parts = []
         for h in range(2):
-            part = ends[:, h * half : (h + 1) * half]
-            part = jnp.where(lane % 2 == 0, pltpu.roll(part, half - 1, 1), pltpu.roll(part, 1, 1))
+            part = jnp.zeros((GROUP, half), jnp.float32)
             for n in range(count // 2):
-                sides[h * count // 2 + n] = pltpu.roll(part, half - 2 * strip * n, 1) if n else part
-        prepare(0)
-
-    def diffuse(s, t, at, under_row):
+                tile = tile_of(h * count // 2 + n)
+                shift = (2 * strip * (n - 2 * g)) % half
+                near = pltpu.roll(tile, shift, 1) if shift else tile
+                shift = (2 * strip * (n - 2 * g - 1)) % half
+                far = pltpu.roll(tile, shift, 1) if shift else tile
+                part = jnp.where(
+                    narrow // (2 * strip) == n, jnp.where(core == 0, near, far), part
+                )
+            parts.append(part)
+        ends.append(jnp.concatenate(parts, axis=1))
+    ends = jnp.concatenate(ends, axis=0)
+    ends = mix_pair(operator, jnp.concatenate([ends, ends], axis=0))[:fields]
+    for h in range(2):
+        part = ends[:, h * half : (h + 1) * half]
+        part = jnp.where(lane % 2 == 0, pltpu.roll(part, half - 1, 1), pltpu.roll(part, 1, 1))
+        for n in range(count // 2):
+            sides[h * count // 2 + n] = pltpu.roll(part, half - 2 * strip * n, 1) if n else part
+    prepare(0)
+
+    def diffuse(s, t, under_row):
         i = s * strip + t + 1
         side = pltpu.roll(sides[s], half - 2 * t - 1, 1)
         for part in range(2):
@@ -366,40 +371,35 @@
                 east = jnp.where(lane == half - 1, side, pltpu.roll(here, half - 1, 1))
             under = mixed[i + 1, :, own] if under_row is None else under_row[:, own]
             around = under + mixed[i - 1, :, own] + east + west
-            out[at, :, own] = here + number * (around - 4.0 * here)
-
-    @pl.loop(0, CHUNK_PAIRS)
-    def _(j):
-        p = step * CHUNK_PAIRS + j
+            out[i - 1, :, own] = here + number * (around - 4.0 * here)
+
+    @pl.loop(0, pairs)
+    def _(p):
         for t in range(2 * strip - 1):
-            diffuse(2 * p + t // strip, t % strip, 2 * strip * j + t, None)
+            diffuse(2 * p + t // strip, t % strip, None)
         head = prepare(jnp.minimum(p + 1, pairs - 1))
         head = jnp.where(p == pairs - 1, mixed[rows + 1], head)
-        diffuse(2 * p + 1, strip - 1, 2 * strip * (j + 1) - 1, head)
-
-
-def step(failed, ocean, sent, strips, operator, number_of):
+        diffuse(2 * p + 1, strip - 1, head)
+
+
+def step(failed, ocean, sent, strips, operator, number_of, *outer):
     rows, fields, columns = ocean.shape
     whole = len(sent) == 1
     pairs = strips.shape[0]
-    chunk = CHUNK_PAIRS * rows // pairs
     return pl.pallas_call(
         functools.partial(step_kernel, whole),
-        grid=(rows // chunk,),
         out_shape=jax.ShapeDtypeStruct(ocean.shape, jnp.float32),
-        in_specs=[SMEM] + [VMEM] * (4 + len(sent)),
-        out_specs=pl.BlockSpec((chunk, fields, columns), lambda g: (g, 0, 0)),
+        in_specs=[SMEM] + [VMEM] * (4 + len(sent) + len(outer)),
+        out_specs=VMEM,
         scratch_shapes=[
             pltpu.VMEM((rows + 2, fields, columns), jnp.float32),
             pltpu.VMEM((2 * pairs, fields, columns // 2), jnp.float32),
         ],
-        compiler_params=pltpu.CompilerParams(
-            vmem_limit_bytes=VMEM_BYTES, dimension_semantics=("arbitrary",)
-        ),
+        compiler_params=pltpu.CompilerParams(vmem_limit_bytes=VMEM_BYTES),
         cost_estimate=pl.CostEstimate(
             flops=100 * ocean.size, bytes_accessed=12 * ocean.size, transcendentals=ocean.size // 2
         ),
-    )(failed, ocean, *sent, strips, operator, number_of)
+    )(failed, ocean, *sent, strips, operator, number_of, *outer)
 
 
 def ends_kernel(stepped, above, under, operator, number_of, out, row, sem):
@@ -462,34 +462,35 @@
         )
     )
     strips = strips.reshape(count, strip, fields, columns)
-    fresh_parity, rebuilt, back, shared = rebuild(failed, weights, strips, saved)
-
-    def finish(ocean, sent, kept):
+    fresh, rebuilt, back, shared = rebuild(failed, weights, strips, saved)
+
+    def exchange_rows(ocean, sent):
         top, bottom = outer_lines(failed, ocean, sent)
         above = lax.ppermute(bottom, "row", [(r, r + 1) for r in range(lines - 1)])
         under = lax.ppermute(top, "row", [(r + 1, r) for r in range(lines - 1)])
-        stepped = step(failed, ocean, sent, *kept)
-        return add_ends(stepped, above, under, *kept[1:])
-
-    def exchange_chips(rebuilt, back, ocean):
+        return above, under
+
+    def exchange_chips(rebuilt, back, ocean, fresh):
         mine = lax.all_to_all(back, ("y_hi", "x"), 0, 0, tiled=True)
         mine, ocean = lax.optimization_barrier((mine, ocean))
         other = lax.ppermute(mine, "core", [(0, 1), (1, 0)])
-        kept = first_half(failed, ocean, mine, op, number, False, count)
+        *kept, parity = first_half(failed, ocean, mine, op, number, fresh, False, count)
         other, kept = lax.optimization_barrier((other, kept))
-        return finish(ocean, (mine, other), kept)
-
-    def exchange_whole(rebuilt, back, ocean):
+        above, under = exchange_rows(ocean, (mine, other))
+        stepped = step(failed, ocean, (mine, other), *kept)
+        return add_ends(stepped, above, under, *kept[1:]), parity
+
+    def exchange_whole(rebuilt, back, ocean, fresh):
         back = spread_whole(failed, rebuilt, back)
         sent = lax.all_to_all(back, MEMBERS, 0, 0, tiled=True)
         sent, ocean = lax.optimization_barrier((sent, ocean))
-        kept = first_half(failed, ocean, sent, op, number, True, count)
-        return finish(ocean, (sent,), kept)
-
-    stepped_state = lax.cond(
-        shared[0] != 0, exchange_whole, exchange_chips, rebuilt, back, ocean
+        above, under = exchange_rows(ocean, (sent,))
+        *kept, parity = first_half(failed, ocean, sent, op, number, fresh, True, count)
+        return step(failed, ocean, (sent,), *kept, above, under), parity
+
+    return lax.cond(
+        shared[0] != 0, exchange_whole, exchange_chips, rebuilt, back, ocean, fresh
     )
-    return stepped_state, fresh_parity
 
 
 def solution(mesh):

time: 115 us -> 96.4 us (0.84)
  blocking collectives: 89.2 us -> 69.9 us
  Pallas kernels: 14.2 us -> 10.6 us
  starting transfers between devices: 8.37 us -> 10.4 us
  local copies, waits for them, and re-layouts: 0.02 us -> 1.68 us
    all_to_all x1, blocking collectives: 44.2 us -> 24.8 us  [exchange_chips(): mine = lax.all_to_all(back, ('y_hi', 'x'), 0, 0, tiled=True)]
    ppermute x2 -> x3, starting transfers between devices: 8.37 us -> 10.4 us  [the longest x1 4.83 us: exchange_rows(): under = lax.ppermute(top, 'row', [(r + 1, r) for r in range(lines - 1)])]
    pallas_call x2 -> x1, Pallas kernels: 5.95 us -> 3.98 us  [step(): pl.pallas_call(functools.partial(step_kernel, whole), out_shape=jax.Shape...]
    unnamed x12 -> x14, local copies, waits for them, and re-layouts: 0.02 us -> 1.68 us
  transfers between devices with their start and end apart: 2 -> 3, of which waited for: 0 -> 1; matrix products, arithmetic and copies ran while one was open for 0% -> 0% of each run, Pallas kernels for 7% -> 7%
where the time goes in v1:
time: 96.4 us; the launch traced here: 94.6 us
  blocking collectives  69.9 us (73%)
  Pallas kernels  10.6 us (11%)
  starting transfers between devices  10.4 us (11%)
  local copies, waits for them, and re-layouts  1.68 us (2%)
  between operations  1.37 us (1%)
    all_to_all x1, blocking collectives, per_device(): strips = lax.all_to_all(ocean_state, MEMBERS, 0, 0, tiled=True)  45.1 us
    all_to_all x1, blocking collectives, exchange_chips(): mine = lax.all_to_all(back, ('y_hi', 'x'), 0, 0, tiled=True)  24.8 us
    ppermute x1, starting transfers between devices, exchange_rows(): under = lax.ppermute(top, 'row', [(r + 1, r) for r in range(lines - 1)])  4.83 us
    pallas_call x1, Pallas kernels, step(): pl.pallas_call(functools.partial(step_kernel, whole), out_shape=jax.Shape...  3.98 us
    ppermute x1, starting transfers between devices, exchange_rows(): above = lax.ppermute(bottom, 'row', [(r, r + 1) for r in range(lines - 1)])  3.55 us
    pallas_call x1, Pallas kernels, rebuild(): pl.pallas_call(rebuild_kernel, out_shape=(jax.ShapeDtypeStruct(saved.shap...  3.22 us
    pallas_call x1, Pallas kernels, first_half(): pl.pallas_call(functools.partial(first_kernel, whole), out_shape=tuple(sh...  2.54 us
    ppermute x1, starting transfers between devices, exchange_chips(): other = lax.ppermute(mine, 'core', [(0, 1), (1, 0)])  2.04 us
  transfers between devices with their start and end apart: 3, of which 1 were waited for; matrix products, arithmetic and copies ran while one was open for 0% of the time, Pallas kernels for 7%

profile of v1, /device:TPU:15, one launch (start us, length us, event | category | flops | bytes accessed | tf_op | source)
XLA Modules:
  0.0 94.6 jit_solution(4953177395191758385)
XLA Ops:
  0.6 0.0 copy-start
  0.6 0.0 copy-start.1
  0.7 0.0 copy-start.4
  0.7 45.1 %all_to_all.15 = f32[128,24,256]{2,1,0:T(8,128)S(1)} all-to-all(f32[128,24,256]{2,1,0:T(8,128)} %param.8), channel_id=1, replica_groups=mesh['row'=8,'y_hi'=2,'x'=4,'core'=2] {'y_hi','x','core'}, dimensions={0} | all-to-all | bytes 6291456 | tf_op jit(solution)/shard_map/all_to_all | solution.py:452
  45.7 0.0 copy-start.2
  45.7 0.0 copy-start.5
  45.7 0.0 copy-start.6
  45.7 0.0 copy-done
  45.7 0.0 copy-done.1
  45.8 0.0 copy-done.4
  45.8 3.2 %shard_map.79 = (f32[8,4,24,256]{3,2,1,0:T(8,128)S(1)}, f32[2,384,128]{2,1,0:T(8,128)S(1)}, f32[8,392,128]{2,1,0:T(8,128)S(1)}, s32[1]{0:T(128)}) custom-call(s32[2,8]{1,0:T(2,128)S(1)} %bitcast.4, s32[4,16]{1,0:T(4,128)S(1)} %copy-done.1, f32[16,8,24,256]{3,2,1,0:T(8,128)S(1)} %bitcast.3, f32[8,4,24,256]{3,2,1,0:T(8,128)S(1)} %copy-done), custom_call_target="tpu_custom_call" | custom-call | flops 6291456 | bytes 4718592 | tf_op jit(solution)/shard_map/pallas_call | solution.py:112
  49.6 0.0 copy-done.2
  49.6 0.0 copy-done.5
  49.7 0.0 copy-done.6
  49.7 43.3 %conditional.1 = (f32[8,4,24,256]{3,2,1,0:T(8,128)}, f32[128,24,256]{2,1,0:T(8,128)S(1)}) conditional(s32[]{:T(128)} %bitcast.2, (f32[8,392,128]{2,1,0:T(8,128)S(1)}, f32[128,24,256]{2,1,0:T(8,128)S(1)}, s32[2,8]{1,0:T(2,128)S(1)}, f32[24,24]{1,0:T(8,128)S(1)}, f32[24]{0:T(128)S(1)}, /*index=5*/f32[8,4,24,256]{3,2,1,0:T(8,128)S(1)}) %tuple.32, ...), branch_computations={%region_0.0_spmd, %region_1.0_spmd} | conditional | flops 137625600 | bytes 22413448 | solution.py:491
  49.7 24.8 %all_to_all.13.sent.refs_0_ = f32[8,392,128]{2,1,0:T(8,128)S(1)} all-to-all(f32[8,392,128]{2,1,0:T(8,128)S(1)} %get-tuple-element.27), channel_id=1, replica_groups=mesh['row'=8,'y_hi'=2,'x'=4,'core'=2] {'y_hi','x'}, dimensions={0} | all-to-all | bytes 3211264 | tf_op jit(solution)/shard_map/cond/branch_0_fun/all_to_all | solution.py:474
  74.5 2.0 %collective-permute-start = (f32[8,392,128]{2,1,0:T(8,128)S(1)}, f32[8,392,128]{2,1,0:T(8,128)S(1)}, u32[]{:S(2)}, u32[]{:S(2)}) collective-permute-start(f32[8,392,128]{2,1,0:T(8,128)S(1)} %all_to_all.13.sent.refs_0_), channel_id=1, source_target_pairs={{0,1},{1,0},{2,3},{3,2},{4,5},{5,4},{6,7},{7,6},{8,9},{9,8},{10,11... | collective-permute-start | bytes 4816904 | tf_op jit(solution)/shard_map/cond/branch_0_fun/ppermute | solution.py:476
  76.5 2.5 %branch_0_fun.4 = (f32[8,8,24,256]{3,2,1,0:T(8,128)S(1)}, bf16[48,144]{1,0:T(8,128)(2,1)S(1)}, f32[24,128]{1,0:T(8,128)S(1)}, f32[8,4,24,256]{3,2,1,0:T(8,128)}) custom-call(s32[2,8]{1,0:T(2,128)S(1)} %get-tuple-element.26.failed, f32[128,24,256]{2,1,0:T(8,128)S(1)} %get-tuple-element.29.ocean, f32[8,392,128]{2,1,0:T(8,128)S(1)} %all_to_all.13.sent.refs_0_, ...), custom_call_target="tpu_custom_call" | custom-call | flops 58982400 | bytes 3145728 | tf_op jit(solution)/shard_map/cond/branch_0_fun/pallas_call | solution.py:277
  79.1 0.5 collective-permute-done.refs_1_
  79.6 0.6 branch_0_fun.6
  80.2 3.5 %collective-permute-start.1 = (f32[48,128]{1,0:T(8,128)S(1)}, f32[48,128]{1,0:T(8,128)S(1)}, u32[]{:S(2)}, u32[]{:S(2)}) collective-permute-start(f32[48,128]{1,0:T(8,128)S(1)} %get-tuple-element.41), channel_id=1, source_target_pairs={{0,16},{16,32},{32,48},{48,64},{64,80},{80,96},{96,112},{1,17},{17... | collective-permute-start | bytes 73736 | tf_op jit(solution)/shard_map/cond/branch_0_fun/ppermute | solution.py:469
  83.8 4.8 %collective-permute-start.2 = (f32[48,128]{1,0:T(8,128)S(1)}, f32[48,128]{1,0:T(8,128)S(1)}, u32[]{:S(2)}, u32[]{:S(2)}) collective-permute-start(f32[48,128]{1,0:T(8,128)S(1)} %get-tuple-element.42), channel_id=1, source_target_pairs={{16,0},{32,16},{48,32},{64,48},{80,64},{96,80},{112,96},{17,1},{33... | collective-permute-start | bytes 73736 | tf_op jit(solution)/shard_map/cond/branch_0_fun/ppermute | solution.py:470
  88.6 4.0 %branch_0_fun.5.stepped = f32[128,24,256]{2,1,0:T(8,128)S(1)} custom-call(s32[2,8]{1,0:T(2,128)S(1)} %get-tuple-element.26.failed, f32[128,24,256]{2,1,0:T(8,128)S(1)} %get-tuple-element.29.ocean, f32[8,392,128]{2,1,0:T(8,128)S(1)} %all_to_all.13.sent.refs_0_, f32[8,392,128]{2,1,0:T(8,128)S(1)} %collective-permute-done.refs_1_, ...), custom_call_target="tpu_custom_call" | custom-call | flops 78643200 | bytes 9437184 | tf_op jit(solution)/shard_map/cond/branch_0_fun/pallas_call | solution.py:389
  92.6 0.0 collective-permute-done.1.above
  92.6 0.0 collective-permute-done.2.under
  92.6 0.3 branch_0_fun.7
  92.9 0.0 copy-start.3
  92.9 1.7 %copy-done.3 = f32[128,24,256]{2,1,0:T(8,128)} copy-done((f32[128,24,256]{2,1,0:T(8,128)}, f32[128,24,256]{2,1,0:T(8,128)S(1)}, u32[]{:S(2)}) %copy-start.3) | copy-done | bytes 3145752
Async XLA Ops:
  0.6 45.1 %copy-start = (f32[8,4,24,256]{3,2,1,0:T(8,128)S(1)}, f32[8,4,24,256]{3,2,1,0:T(8,128)}, u32[]{:S(2)}) copy-start(f32[8,4,24,256]{3,2,1,0:T(8,128)} %saved) | copy-start | bytes 2359300
  0.6 45.1 %copy-start.1 = (s32[4,16]{1,0:T(4,128)S(1)}, s32[4,16]{1,0:T(4,128)}, u32[]{:S(2)}) copy-start(s32[4,16]{1,0:T(4,128)} %weights) | copy-start | bytes 772
  0.7 45.1 %copy-start.4 = (s32[8,2]{0,1:T(2,128)S(1)}, s32[8,2]{0,1:T(2,128)}, u32[]{:S(2)}) copy-start(s32[8,2]{0,1:T(2,128)} %param.11) | copy-start | bytes 196
  45.7 3.9 %copy-start.2 = (f32[128,24,256]{2,1,0:T(8,128)S(1)}, f32[128,24,256]{2,1,0:T(8,128)}, u32[]{:S(2)}) copy-start(f32[128,24,256]{2,1,0:T(8,128)} %param.8) | copy-start | bytes 9437188
  45.7 3.9 %copy-start.5 = (f32[24,24]{1,0:T(8,128)S(1)}, f32[24,24]{1,0:T(8,128)}, u32[]{:S(2)}) copy-start(f32[24,24]{1,0:T(8,128)} %param.12) | copy-start | bytes 6916
  45.7 3.9 %copy-start.6 = (f32[24]{0:T(128)S(1)}, f32[24]{0:T(128)}, u32[]{:S(2)}) copy-start(f32[24]{0:T(128)} %param.13) | copy-start | bytes 292
  74.5 5.1 %collective-permute-start = (f32[8,392,128]{2,1,0:T(8,128)S(1)}, f32[8,392,128]{2,1,0:T(8,128)S(1)}, u32[]{:S(2)}, u32[]{:S(2)}) collective-permute-start(f32[8,392,128]{2,1,0:T(8,128)S(1)} %all_to_all.13.sent.refs_0_), channel_id=1, source_target_pairs={{0,1},{1,0},{2,3},{3,2},{4,5},{5,4},{6,7},{7,6},{8,9},{9,8},{10,11... | collective-permute-start | bytes 4816904 | tf_op jit(solution)/shard_map/cond/branch_0_fun/ppermute | solution.py:476
  80.2 12.4 %collective-permute-start.1 = (f32[48,128]{1,0:T(8,128)S(1)}, f32[48,128]{1,0:T(8,128)S(1)}, u32[]{:S(2)}, u32[]{:S(2)}) collective-permute-start(f32[48,128]{1,0:T(8,128)S(1)} %get-tuple-element.41), channel_id=1, source_target_pairs={{0,16},{16,32},{32,48},{48,64},{64,80},{80,96},{96,112},{1,17},{17... | collective-permute-start | bytes 73736 | tf_op jit(solution)/shard_map/cond/branch_0_fun/ppermute | solution.py:469
  83.8 8.8 %collective-permute-start.2 = (f32[48,128]{1,0:T(8,128)S(1)}, f32[48,128]{1,0:T(8,128)S(1)}, u32[]{:S(2)}, u32[]{:S(2)}) collective-permute-start(f32[48,128]{1,0:T(8,128)S(1)} %get-tuple-element.42), channel_id=1, source_target_pairs={{16,0},{32,16},{48,32},{64,48},{80,64},{96,80},{112,96},{17,1},{33... | collective-permute-start | bytes 73736 | tf_op jit(solution)/shard_map/cond/branch_0_fun/ppermute | solution.py:470
  92.9 1.7 %copy-start.3 = (f32[128,24,256]{2,1,0:T(8,128)}, f32[128,24,256]{2,1,0:T(8,128)S(1)}, u32[]{:S(2)}) copy-start(f32[128,24,256]{2,1,0:T(8,128)S(1)} %get-tuple-element.83) | copy-start | bytes 9437188

commit v2 on v1

--- a/solution.py
+++ b/solution.py
@@ -58,9 +58,8 @@
         ends = pltpu.roll(jnp.where(lane == 0, first, final), 2 * i + 1, 1)
         edges[n] = jnp.where((lane == 2 * i) | (lane == 2 * i + 1), ends, edges[n])
 
-    @pl.loop(0, rows)
-    def _(i):
-        at = pl.multiple_of(i * wide, 8)
+    for i in range(rows):
+        at = i * wide
         living = [None] * checks
         for c in range(count):
             block = strips[c, i]
@@ -252,7 +251,7 @@
         number = jnp.where(field == f, diffusivity[f], number)
     number_of[...] = number
 
-    @pl.loop(0, count // 2)
+    @pl.loop(0, count // 2, unroll=4)
     def _(p):
         s = 2 * p + core
         at = s if whole else p

time: 96.4 us -> 112 us (1.16)
  blocking collectives: 69.9 us -> 89.2 us
  starting transfers between devices: 10.4 us -> 8.37 us
    all_to_all x1, blocking collectives: 24.8 us -> 44.2 us  [exchange_whole(): sent = lax.all_to_all(back, MEMBERS, 0, 0, tiled=True)]
    ppermute x1 -> x0, starting transfers between devices: 2.04 us -> none  [exchange_chips(): other = lax.ppermute(mine, 'core', [(0, 1), (1, 0)])]
  transfers between devices with their start and end apart: 3 -> 2, of which waited for: 1 -> 0; matrix products, arithmetic and copies ran while one was open for 0% -> 0% of each run, Pallas kernels for 7% -> 2%
where the time goes in v2:
time: 112 us; the launch traced here: 110 us
  blocking collectives  89.2 us (80%)
  Pallas kernels  9.63 us (9%)
  starting transfers between devices  8.37 us (7%)
  local copies, waits for them, and re-layouts  1.68 us (2%)
  between operations  1.37 us (1%)
    all_to_all x1, blocking collectives, per_device(): strips = lax.all_to_all(ocean_state, MEMBERS, 0, 0, tiled=True)  45.1 us
    all_to_all x1, blocking collectives, exchange_whole(): sent = lax.all_to_all(back, MEMBERS, 0, 0, tiled=True)  44.2 us
    ppermute x1, starting transfers between devices, exchange_rows(): under = lax.ppermute(top, 'row', [(r + 1, r) for r in range(lines - 1)])  4.83 us
    pallas_call x1, Pallas kernels, step(): pl.pallas_call(functools.partial(step_kernel, whole), out_shape=jax.Shape...  3.98 us
    ppermute x1, starting transfers between devices, exchange_rows(): above = lax.ppermute(bottom, 'row', [(r, r + 1) for r in range(lines - 1)])  3.55 us
    pallas_call x1, Pallas kernels, rebuild(): pl.pallas_call(rebuild_kernel, out_shape=(jax.ShapeDtypeStruct(saved.shap...  2.52 us
  transfers between devices with their start and end apart: 2, of which 0 were waited for; matrix products, arithmetic and copies ran while one was open for 0% of the time, Pallas kernels for 2%

profile of v2, /device:TPU:15, one launch (start us, length us, event | category | flops | bytes accessed | tf_op | source)
XLA Modules:
  0.0 110.4 jit_solution(186560245473083543)
XLA Ops:
  0.6 0.0 copy-start
  0.6 0.0 copy-start.1
  0.7 0.0 copy-start.4
  0.7 45.1 %all_to_all.15 = f32[128,24,256]{2,1,0:T(8,128)S(1)} all-to-all(f32[128,24,256]{2,1,0:T(8,128)} %param.8), channel_id=1, replica_groups=mesh['row'=8,'y_hi'=2,'x'=4,'core'=2] {'y_hi','x','core'}, dimensions={0} | all-to-all | bytes 6291456 | tf_op jit(solution)/shard_map/all_to_all | solution.py:451
  45.7 0.0 copy-start.2
  45.7 0.0 copy-start.5
  45.7 0.0 copy-start.6
  45.7 0.0 copy-done
  45.7 0.0 copy-done.1
  45.8 0.0 copy-done.4
  45.8 2.5 %shard_map.79 = (f32[8,4,24,256]{3,2,1,0:T(8,128)S(1)}, f32[2,384,128]{2,1,0:T(8,128)S(1)}, f32[8,392,128]{2,1,0:T(8,128)S(1)}, s32[1]{0:T(128)}) custom-call(s32[2,8]{1,0:T(2,128)S(1)} %bitcast.4, s32[4,16]{1,0:T(4,128)S(1)} %copy-done.1, f32[16,8,24,256]{3,2,1,0:T(8,128)S(1)} %bitcast.3, f32[8,4,24,256]{3,2,1,0:T(8,128)S(1)} %copy-done), custom_call_target="tpu_custom_call" | custom-call | flops 6291456 | bytes 4718592 | tf_op jit(solution)/shard_map/pallas_call | solution.py:111
  48.9 0.0 copy-done.2
  48.9 0.0 copy-done.5
  49.0 0.0 copy-done.6
  49.0 59.7 %conditional.1 = (f32[8,4,24,256]{3,2,1,0:T(8,128)}, f32[128,24,256]{2,1,0:T(8,128)S(1)}) conditional(s32[]{:T(128)} %bitcast.2, (f32[8,392,128]{2,1,0:T(8,128)S(1)}, f32[128,24,256]{2,1,0:T(8,128)S(1)}, s32[2,8]{1,0:T(2,128)S(1)}, f32[24,24]{1,0:T(8,128)S(1)}, f32[24]{0:T(128)S(1)}, /*index=5*/f32[8,4,24,256]{3,2,1,0:T(8,128)S(1)}) %tuple.32, ...), branch_computations={%region_0.0_spmd, %region_1.0_spmd} | conditional | flops 137625600 | bytes 22413448 | solution.py:490
  49.0 0.8 branch_1_fun.4
  49.8 44.2 %all_to_all.14.sent.refs_0_ = f32[16,392,128]{2,1,0:T(8,128)S(1)} all-to-all(f32[16,392,128]{2,1,0:T(8,128)S(1)} %branch_1_fun.4), channel_id=1, replica_groups=mesh['row'=8,'y_hi'=2,'x'=4,'core'=2] {'y_hi','x','core'}, dimensions={0} | all-to-all | bytes 6422528 | tf_op jit(solution)/shard_map/cond/branch_1_fun/all_to_all | solution.py:484
  94.0 0.6 branch_1_fun.6
  94.6 3.5 %collective-permute-start.3 = (f32[48,128]{1,0:T(8,128)S(1)}, f32[48,128]{1,0:T(8,128)S(1)}, u32[]{:S(2)}, u32[]{:S(2)}) collective-permute-start(f32[48,128]{1,0:T(8,128)S(1)} %get-tuple-element.56), channel_id=1, source_target_pairs={{0,16},{16,32},{32,48},{48,64},{64,80},{80,96},{96,112},{1,17},{17... | collective-permute-start | bytes 73736 | tf_op jit(solution)/shard_map/cond/branch_1_fun/ppermute | solution.py:468
  98.1 4.8 %collective-permute-start.4 = (f32[48,128]{1,0:T(8,128)S(1)}, f32[48,128]{1,0:T(8,128)S(1)}, u32[]{:S(2)}, u32[]{:S(2)}) collective-permute-start(f32[48,128]{1,0:T(8,128)S(1)} %get-tuple-element.57), channel_id=1, source_target_pairs={{16,0},{32,16},{48,32},{64,48},{80,64},{96,80},{112,96},{17,1},{33... | collective-permute-start | bytes 73736 | tf_op jit(solution)/shard_map/cond/branch_1_fun/ppermute | solution.py:469
  103.0 1.7 %branch_1_fun.5 = (f32[8,8,24,256]{3,2,1,0:T(8,128)S(1)}, bf16[48,144]{1,0:T(8,128)(2,1)S(1)}, f32[24,128]{1,0:T(8,128)S(1)}, f32[8,4,24,256]{3,2,1,0:T(8,128)}) custom-call(s32[2,8]{1,0:T(2,128)S(1)} %get-tuple-element.44.failed, f32[128,24,256]{2,1,0:T(8,128)S(1)} %get-tuple-element.48.ocean, f32[16,392,128]{2,1,0:T(8,128)S(1)} %all_to_all.14.sent.refs_0_, ...), custom_call_target="tpu_custom_call" | custom-call | flops 58982400 | bytes 3145728 | tf_op jit(solution)/shard_map/cond/branch_1_fun/pallas_call | solution.py:276
  104.7 0.0 collective-permute-done.3.refs_4_
  104.7 0.0 collective-permute-done.4.refs_5_
  104.7 4.0 %branch_1_fun.7 = f32[128,24,256]{2,1,0:T(8,128)S(1)} custom-call(s32[2,8]{1,0:T(2,128)S(1)} %get-tuple-element.44.failed, f32[128,24,256]{2,1,0:T(8,128)S(1)} %get-tuple-element.48.ocean, f32[16,392,128]{2,1,0:T(8,128)S(1)} %all_to_all.14.sent.refs_0_, f32[8,8,24,256]{3,2,1,0:T(8,128)S(1)} %get-tuple-element.53.refs_1_, ...), custom_call_target="tpu_custom_call" | custom-call | flops 78643200 | bytes 9437184 | tf_op jit(solution)/shard_map/cond/branch_1_fun/pallas_call | solution.py:388
  108.7 0.0 copy-start.3
  108.7 1.7 %copy-done.3 = f32[128,24,256]{2,1,0:T(8,128)} copy-done((f32[128,24,256]{2,1,0:T(8,128)}, f32[128,24,256]{2,1,0:T(8,128)S(1)}, u32[]{:S(2)}) %copy-start.3) | copy-done | bytes 3145752
Async XLA Ops:
  0.6 45.1 %copy-start = (f32[8,4,24,256]{3,2,1,0:T(8,128)S(1)}, f32[8,4,24,256]{3,2,1,0:T(8,128)}, u32[]{:S(2)}) copy-start(f32[8,4,24,256]{3,2,1,0:T(8,128)} %saved) | copy-start | bytes 2359300
  0.6 45.1 %copy-start.1 = (s32[4,16]{1,0:T(4,128)S(1)}, s32[4,16]{1,0:T(4,128)}, u32[]{:S(2)}) copy-start(s32[4,16]{1,0:T(4,128)} %weights) | copy-start | bytes 772
  0.7 45.1 %copy-start.4 = (s32[8,2]{0,1:T(2,128)S(1)}, s32[8,2]{0,1:T(2,128)}, u32[]{:S(2)}) copy-start(s32[8,2]{0,1:T(2,128)} %param.11) | copy-start | bytes 196
  45.7 3.2 %copy-start.2 = (f32[128,24,256]{2,1,0:T(8,128)S(1)}, f32[128,24,256]{2,1,0:T(8,128)}, u32[]{:S(2)}) copy-start(f32[128,24,256]{2,1,0:T(8,128)} %param.8) | copy-start | bytes 9437188
  45.7 3.2 %copy-start.5 = (f32[24,24]{1,0:T(8,128)S(1)}, f32[24,24]{1,0:T(8,128)}, u32[]{:S(2)}) copy-start(f32[24,24]{1,0:T(8,128)} %param.12) | copy-start | bytes 6916
  45.7 3.2 %copy-start.6 = (f32[24]{0:T(128)S(1)}, f32[24]{0:T(128)}, u32[]{:S(2)}) copy-start(f32[24]{0:T(128)} %param.13) | copy-start | bytes 292
  94.6 10.1 %collective-permute-start.3 = (f32[48,128]{1,0:T(8,128)S(1)}, f32[48,128]{1,0:T(8,128)S(1)}, u32[]{:S(2)}, u32[]{:S(2)}) collective-permute-start(f32[48,128]{1,0:T(8,128)S(1)} %get-tuple-element.56), channel_id=1, source_target_pairs={{0,16},{16,32},{32,48},{48,64},{64,80},{80,96},{96,112},{1,17},{17... | collective-permute-start | bytes 73736 | tf_op jit(solution)/shard_map/cond/branch_1_fun/ppermute | solution.py:468
  98.1 6.6 %collective-permute-start.4 = (f32[48,128]{1,0:T(8,128)S(1)}, f32[48,128]{1,0:T(8,128)S(1)}, u32[]{:S(2)}, u32[]{:S(2)}) collective-permute-start(f32[48,128]{1,0:T(8,128)S(1)} %get-tuple-element.57), channel_id=1, source_target_pairs={{16,0},{32,16},{48,32},{64,48},{80,64},{96,80},{112,96},{17,1},{33... | collective-permute-start | bytes 73736 | tf_op jit(solution)/shard_map/cond/branch_1_fun/ppermute | solution.py:469
  108.7 1.7 %copy-start.3 = (f32[128,24,256]{2,1,0:T(8,128)}, f32[128,24,256]{2,1,0:T(8,128)S(1)}, u32[]{:S(2)}) copy-start(f32[128,24,256]{2,1,0:T(8,128)S(1)} %get-tuple-element.83) | copy-start | bytes 9437188
